TPU v7x, 32 devices: a whole 2x2x4 slice. The times are simulated.
32 devices in a mesh: ctx: 8 (over z, x), vis: 4 (over y, core).
Axes of the slice: x: 2, y: 2, z: 4, core: 2. Of those that a mesh axis runs over, the one named last changes fastest.
Arguments:
- features: bfloat16 [8, 256, 1536], P('ctx'), may hold values from -6 to 6
- latent_init: bfloat16 [64, 1536], replicated, may hold values from -6 to 6
- feat_gain: float32 [1536], replicated, may hold values from 0.25 to 1.75
- latent_gain: float32 [1536], replicated, may hold values from 0.25 to 1.75
- resamp_query: bfloat16 [1536, 512], P(None, 'vis'), may hold values from -0.15625 to 0.15625
- resamp_key: bfloat16 [1536, 512], P(None, 'vis'), may hold values from -0.15625 to 0.15625
- resamp_value: bfloat16 [1536, 512], P(None, 'vis'), may hold values from -0.15625 to 0.15625
- resampler_output_weight: bfloat16 [512, 1536], P('vis'), may hold values from -0.25 to 0.25
- cross_key_weight: bfloat16 [1536, 4096], P(None, 'vis'), may hold values from -0.15625 to 0.15625
- cross_value_weight: bfloat16 [1536, 4096], P(None, 'vis'), may hold values from -0.15625 to 0.15625
- slot_image: int32 [8], replicated, may hold values from 0 to 7, each once
- segments: int32 [2048], replicated, may hold values from 0 to 7, as said below
- latest_image: int32 [2048], P('ctx'), may hold values from -1 to 7, as said below
- cross_query: bfloat16 [2048, 4096], P('ctx', 'vis'), may hold values from -6 to 6
- self_query: bfloat16 [2048, 4096], P('ctx', 'vis'), may hold values from -64 to 64
- self_key: bfloat16 [2048, 4096], P('ctx', 'vis'), may hold values from -6 to 6
- self_value: bfloat16 [2048, 4096], P('ctx', 'vis'), may hold values from -6 to 6
- cross_gate: float32 [32], P('vis'), may hold values from 0.3 to 1.5
- grad_output: bfloat16 [2048, 4096], P('ctx', 'vis'), may hold values from -6 to 6
Outputs:
- attended: bfloat16 [2048, 4096], P('ctx', 'vis')
- grad_query: bfloat16 [2048, 4096], P('ctx', 'vis')
- grad_key: bfloat16 [2048, 4096], P('ctx', 'vis')
- grad_value: bfloat16 [2048, 4096], P('ctx', 'vis')
- grad_cross_query: bfloat16 [2048, 4096], P('ctx', 'vis')
- grad_latents: bfloat16 [8, 64, 1536], P('ctx', None, 'vis')
Inputs may be any that keep to these rules, and one draw needn't show every extreme that they name: `segments`: documents are numbered in order of position, token 0 begins document 0. `latest_image`: images are numbered in order of position; token 0 has -1.
All inputs are finite; a program needn't handle non-finite values.
Results may differ from a plain program's by a relative error of at most 0.019.
Values may be sent and summed in bfloat16 or wider, within the bound.
A program may use at most 192 MiB of HBM per device.

v0:
```python
import math

import jax
import jax.numpy as jnp
from jax import lax
from jax.sharding import PartitionSpec as P

LATENT_COUNT = 64
RESAMPLER_WIDTH = 64
DH = 128


def layer_norm(values, norm_gain):
    center = jnp.mean(values, axis=-1, keepdims=True)
    spread = jnp.mean((values - center) ** 2, axis=-1, keepdims=True)
    return ((values - center) * lax.rsqrt(spread + 1e-05) * norm_gain).astype(jnp.bfloat16)


def masked_softmax(scores, allowed):
    masked = jnp.where(allowed, scores, jnp.float32(-1e30))
    peak = jnp.max(masked, axis=-1, keepdims=True)
    raised = jnp.where(allowed, jnp.exp(masked - peak), jnp.float32(0.0))
    summed = jnp.sum(raised, axis=-1, keepdims=True)
    return raised / jnp.where(summed > 0, summed, jnp.float32(1.0))


def shards(
    features,
    latent_init,
    feat_gain,
    latent_gain,
    resamp_query,
    resamp_key,
    resamp_value,
    resampler_output_weight,
    cross_key_weight,
    cross_value_weight,
    slot_image,
    segments,
    latest_image,
    cross_query,
    self_query,
    self_key,
    self_value,
    cross_gate,
    grad_output,
):
    single_float = jnp.float32
    brain_float_half = jnp.bfloat16
    shard_at = lax.axis_index("ctx")
    local_rows = self_query.shape[0]
    head_columns = self_query.shape[1]
    local_heads = cross_gate.shape[0]
    score_scale = 1.0 / math.sqrt(DH)
    slots_here = features.shape[0]
    feat_rows = features.shape[1]
    feat_norm = layer_norm(features.astype(single_float), feat_gain)
    lat_norm = layer_norm(latent_init.astype(single_float), latent_gain)
    res_heads = resamp_query.shape[1] // RESAMPLER_WIDTH
    res_q = jnp.dot(lat_norm, resamp_query, preferred_element_type=single_float).astype(
        brain_float_half
    )
    joined = jnp.concatenate([feat_norm, lat_norm[None]], axis=1)
    res_k = jnp.einsum(
        "sfd,de->sfe", joined, resamp_key, preferred_element_type=single_float
    ).astype(brain_float_half)
    res_v = jnp.einsum(
        "sfd,de->sfe", joined, resamp_value, preferred_element_type=single_float
    ).astype(brain_float_half)
    joined_rows = feat_rows + LATENT_COUNT
    res_score = jnp.einsum(
        "nhe,sfhe->shnf",
        res_q.reshape(LATENT_COUNT, res_heads, RESAMPLER_WIDTH),
        res_k.reshape(slots_here, joined_rows, res_heads, RESAMPLER_WIDTH),
        preferred_element_type=single_float,
    ) / math.sqrt(RESAMPLER_WIDTH)
    res_prob = jax.nn.softmax(res_score, axis=-1).astype(brain_float_half)
    resampler_mixture = jnp.einsum(
        "shnf,sfhe->snhe",
        res_prob,
        res_v.reshape(slots_here, joined_rows, res_heads, RESAMPLER_WIDTH),
        preferred_element_type=single_float,
    ).astype(brain_float_half)
    partial_out = jnp.einsum(
        "uxt,th->uxh",
        resampler_mixture.reshape(slots_here, LATENT_COUNT, res_heads * RESAMPLER_WIDTH),
        resampler_output_weight,
        preferred_element_type=single_float,
    )
    resampled = lax.psum(partial_out, "vis")
    latent_rows = (latent_init.astype(single_float)[None] + resampled).astype(brain_float_half)
    latent_stack = lax.all_gather(latent_rows, "ctx", axis=0, tiled=True)
    cross_key_rows = jnp.einsum(
        "qzv,vc->qzc", latent_stack, cross_key_weight, preferred_element_type=single_float
    ).astype(brain_float_half)
    cross_value_rows = jnp.einsum(
        "qzv,vc->qzc", latent_stack, cross_value_weight, preferred_element_type=single_float
    ).astype(brain_float_half)
    all_slots = cross_key_rows.shape[0]
    key_count = all_slots * LATENT_COUNT
    xkey_rows = cross_key_rows.reshape(key_count, local_heads, DH)
    xvalue_rows = cross_value_rows.reshape(key_count, local_heads, DH)
    col_image = jnp.repeat(slot_image, LATENT_COUNT)
    cquery_rows = cross_query.reshape(local_rows, local_heads, DH)
    cross_allowed = (col_image[None, :] == latest_image[:, None])[None]
    c_prob = masked_softmax(
        jnp.einsum("thd,khd->htk", cquery_rows, xkey_rows, preferred_element_type=single_float)
        * score_scale,
        cross_allowed,
    )
    c_half = c_prob.astype(brain_float_half)
    cross = jnp.einsum("htk,khd->thd", c_half, xvalue_rows, preferred_element_type=single_float)
    gate_tanh = jnp.tanh(cross_gate)[None, :, None]
    value_in = (
        self_value.reshape(local_rows, local_heads, DH).astype(single_float) + gate_tanh * cross
    ).astype(brain_float_half)
    keys_all, values_all = (
        lax.all_gather(self_key, "ctx", axis=0, tiled=True),
        lax.all_gather(value_in.reshape(local_rows, head_columns), "ctx", axis=0, tiled=True),
    )
    total_rows = keys_all.shape[0]
    keys_all = keys_all.reshape(total_rows, local_heads, DH)
    values_all = values_all.reshape(total_rows, local_heads, DH)
    query_rows = self_query.reshape(local_rows, local_heads, DH)
    grad_rows = grad_output.reshape(local_rows, local_heads, DH)
    query_pos = shard_at * local_rows + jnp.arange(local_rows, dtype=jnp.int32)
    key_pos = jnp.arange(total_rows, dtype=jnp.int32)
    query_seg = lax.dynamic_slice_in_dim(segments, shard_at * local_rows, local_rows, 0)
    self_allowed = (
        (query_seg[:, None] == segments[None, :]) & (key_pos[None, :] <= query_pos[:, None])
    )[None]
    self_score = (
        jnp.einsum("thd,khd->htk", query_rows, keys_all, preferred_element_type=single_float)
        * score_scale
    )
    s_prob = masked_softmax(self_score, self_allowed)
    s_half = s_prob.astype(brain_float_half)
    attended = (
        jnp.einsum("htk,khd->thd", s_half, values_all, preferred_element_type=single_float)
        .astype(brain_float_half)
        .reshape(local_rows, head_columns)
    )
    d_prob = jnp.einsum("thd,khd->htk", grad_rows, values_all, preferred_element_type=single_float)
    row_delta = jnp.sum(s_prob * d_prob, axis=-1)
    d_score = (s_prob * (d_prob - row_delta[..., None]) * score_scale).astype(brain_float_half)
    grad_query = (
        jnp.einsum("htk,khd->thd", d_score, keys_all, preferred_element_type=single_float)
        .astype(brain_float_half)
        .reshape(local_rows, head_columns)
    )
    masked_score = jnp.where(self_allowed, self_score, single_float(-1e30))
    row_peak = jnp.max(masked_score, axis=-1)
    row_total = jnp.sum(
        jnp.where(self_allowed, jnp.exp(masked_score - row_peak[..., None]), single_float(0.0)),
        axis=-1,
    )
    log_total = row_peak + jnp.log(row_total)
    query_all, grad_all = (
        lax.all_gather(self_query, "ctx", axis=0, tiled=True),
        lax.all_gather(grad_output, "ctx", axis=0, tiled=True),
    )
    lse_all, delta_all = (
        lax.all_gather(log_total.T, "ctx", axis=0, tiled=True),
        lax.all_gather(row_delta.T, "ctx", axis=0, tiled=True),
    )
    query_all = query_all.reshape(total_rows, local_heads, DH)
    grad_all = grad_all.reshape(total_rows, local_heads, DH)
    own_keys = self_key.reshape(local_rows, local_heads, DH)
    owned_allowed = (
        (segments[:, None] == query_seg[None, :]) & (query_pos[None, :] <= key_pos[:, None])
    )[None]
    back_score = (
        jnp.einsum("qhd,khd->hqk", query_all, own_keys, preferred_element_type=single_float)
        * score_scale
    )
    back_prob = jnp.exp(
        jnp.where(owned_allowed, back_score - lse_all.T[:, :, None], single_float(-1e30))
    )
    back_prob = jnp.where(owned_allowed, back_prob, single_float(0.0))
    back_half = back_prob.astype(brain_float_half)
    back_dprob = jnp.einsum("qhd,khd->hqk", grad_all, value_in, preferred_element_type=single_float)
    back_dscore = (back_prob * (back_dprob - delta_all.T[:, :, None]) * score_scale).astype(
        brain_float_half
    )
    key_sum = jnp.einsum(
        "hqk,qhd->khd", back_dscore, query_all, preferred_element_type=single_float
    ).reshape(local_rows, head_columns)
    vin_sum = jnp.einsum(
        "hqk,qhd->khd", back_half, grad_all, preferred_element_type=single_float
    ).reshape(local_rows, head_columns)
    grad_key = key_sum.astype(brain_float_half)
    grad_value = vin_sum.astype(brain_float_half)
    d_cross = (gate_tanh * vin_sum.reshape(local_rows, local_heads, DH)).astype(brain_float_half)
    c_dprob = jnp.einsum("thd,khd->htk", d_cross, xvalue_rows, preferred_element_type=single_float)
    c_score = (
        c_prob * (c_dprob - jnp.sum(c_prob * c_dprob, axis=-1, keepdims=True)) * score_scale
    ).astype(brain_float_half)
    grad_cross_query = (
        jnp.einsum("htk,khd->thd", c_score, xkey_rows, preferred_element_type=single_float)
        .astype(brain_float_half)
        .reshape(local_rows, head_columns)
    )
    grad_xk = jnp.einsum("htk,thd->khd", c_score, cquery_rows, preferred_element_type=single_float)
    grad_xv = jnp.einsum("htk,thd->khd", c_half, d_cross, preferred_element_type=single_float)
    stacked = jnp.concatenate(
        [
            grad_xk.reshape(all_slots, LATENT_COUNT, head_columns),
            grad_xv.reshape(all_slots, LATENT_COUNT, head_columns),
        ],
        axis=2,
    )
    local_gradients = lax.psum_scatter(stacked, "ctx", scatter_dimension=0, tiled=True).astype(
        brain_float_half
    )
    latent_part = jnp.einsum(
        "zmx,tx->zmt",
        local_gradients[:, :, :head_columns],
        cross_key_weight,
        preferred_element_type=single_float,
    )
    latent_part = latent_part + jnp.einsum(
        "zmx,tx->zmt",
        local_gradients[:, :, head_columns:],
        cross_value_weight,
        preferred_element_type=single_float,
    )
    grad_latents = lax.psum_scatter(latent_part, "vis", scatter_dimension=2, tiled=True).astype(
        brain_float_half
    )
    return (attended, grad_query, grad_key, grad_value, grad_cross_query, grad_latents)


def solution(mesh):
    in_specs = (
        P("ctx", None, None),
        P(),
        P(),
        P(),
        P(None, "vis"),
        P(None, "vis"),
        P(None, "vis"),
        P("vis", None),
        P(None, "vis"),
        P(None, "vis"),
        P(),
        P(),
        P("ctx"),
        P("ctx", "vis"),
        P("ctx", "vis"),
        P("ctx", "vis"),
        P("ctx", "vis"),
        P("vis"),
        P("ctx", "vis"),
    )
    out_specs = (
        P("ctx", "vis"),
        P("ctx", "vis"),
        P("ctx", "vis"),
        P("ctx", "vis"),
        P("ctx", "vis"),
        P("ctx", None, "vis"),
    )
    return jax.shard_map(shards, mesh=mesh, in_specs=in_specs, out_specs=out_specs, check_vma=False)
```

profile of v0, /device:TPU:0, one launch (start us, length us, event | category | flops | bytes accessed | tf_op | source)
XLA Modules:
  0.0 540.0 jit_solution(12080464674861063833)
XLA Ops:
  28.0 35.4 %all-reduce.2.cloned.1.call-done = f32[1,64,1536]{2,1,0:T(8,128)} async-done(((f32[1,64,1536]{2,1,0:T(8,128)}), f32[1,64,1536]{2,1,0:T(8,128)}) %all-reduce.2.cloned.1.call-update) | async-done | bytes 393232 | tf_op jit(solution)/shard_map/psum | solution.py:90
  74.2 36.4 %all-gather.6.cloned.1.call-done = bf16[8,64,1536]{2,1,0:T(8,128)(2,1)} async-done(((bf16[1,64,1536]{2,1,0:T(8,128)(2,1)}), bf16[8,64,1536]{2,1,0:T(8,128)(2,1)}) %all-gather.6.cloned.1.call-update) | async-done | bytes 1572880 | tf_op jit(solution)/shard_map/all_gather | solution.py:92
  110.6 4.3 fusion.56
  131.3 56.0 %all-gather.10.cloned.1.call-done = bf16[2048,1024]{0,1:T(8,128)(2,1)} async-done(((bf16[256,1024]{0,1:T(8,128)(2,1)}), bf16[2048,1024]{0,1:T(8,128)(2,1)}) %all-gather.10.cloned.1.call-update) | async-done | bytes 4194320 | tf_op jit(solution)/shard_map/all_gather | solution.py:118
  187.3 5.5 %fusion.8 = (f32[8,256]{1,0:T(8,128)S(1)}, f32[8,256,2048]{2,1,0:T(8,128)S(1)}) fusion(pred[256,2048]{1,0:T(8,128)(4,1)} %fusion.45, bf16[2048,8,128]{0,2,1:T(8,128)(2,1)} %bitcast.185, bf16[256,1024]{1,0:T(8,128)(2,1)} %param.33), kind=kOutput, calls=%fused_computation.14 | convolution fusion | flops 1086322688 | bytes 22028288 | tf_op jit(solution)/shard_map/thd,khd->htk/dot_general | solution.py:133
  192.8 5.0 fusion.10
  198.9 30.8 %all_gather.25 = f32[2048,8]{0,1:T(8,128)S(1)} all-gather(f32[256,8]{0,1:T(8,128)S(1)} %get-tuple-element.30), channel_id=1, replica_groups=mesh['ctx'=8,'vis'=4] {'ctx'}, dimensions={0}, use_global_device_ids=true | all-gather | bytes 73728 | tf_op jit(solution)/shard_map/all_gather | solution.py:163
  229.7 33.9 %all-gather.12.cloned.1.call-done = bf16[2048,1024]{0,1:T(8,128)(2,1)} async-done(((bf16[256,1024]{0,1:T(8,128)(2,1)}), bf16[2048,1024]{0,1:T(8,128)(2,1)}) %all-gather.12.cloned.1.call-update) | async-done | bytes 4194320 | tf_op jit(solution)/shard_map/all_gather | solution.py:159
  263.6 10.8 %fusion.84 = f32[8,2048,256]{2,1,0:T(8,128)} fusion(bf16[2048,8,128]{0,2,1:T(8,128)(2,1)} %bitcast.190, bf16[256,1024]{1,0:T(8,128)(2,1)} %param.34), kind=kOutput, calls=%fused_computation.90 | convolution fusion | flops 1073741824 | bytes 21495808 | tf_op jit(solution)/shard_map/qhd,khd->hqk/dot_general | solution.py:173
  274.4 64.6 %all-gather.14.cloned.1.call-done = bf16[2048,1024]{0,1:T(8,128)(2,1)} async-done(((bf16[256,1024]{0,1:T(8,128)(2,1)}), bf16[2048,1024]{0,1:T(8,128)(2,1)}) %all-gather.14.cloned.1.call-update) | async-done | bytes 4194320 | tf_op jit(solution)/shard_map/all_gather | solution.py:160
  339.0 10.5 %fusion.132 = (bf16[8,256,128]{1,2,0:T(8,128)(2,1)}, f32[8,256,128]{1,2,0:T(8,128)}) fusion(bf16[2048,8,128]{0,2,1:T(8,128)(2,1)} %bitcast.208, f32[8,2048,256]{2,1,0:T(8,128)} %fusion.84, f32[8,2048]{1,0:T(8,128)S(1)} %bitcast.203, pred[2048,256]{1,0:T(8,128)(4,1)} %fusion.46), kind=kOutput, calls=%fused_computation.146 | convolution fusion | flops 1094975488 | bytes 23134208 | tf_op jit(solution)/shard_map/hqk,qhd->khd/dot_general | solution.py:188
  351.5 4.3 fusion.81
  355.8 8.5 %fusion.71 = bf16[8,128,256]{2,1,0:T(8,128)(2,1)} fusion(bf16[512,8,128]{0,2,1:T(8,128)(2,1)} %copy.147, f32[8,256,512]{1,2,0:T(8,128)} %fusion.81, f32[8,256,512]{1,2,0:T(8,128)} %copy-done.16, f32[8,256]{1,0:T(8,128)S(1)} %compare_select_fusion.1), kind=kOutput, calls=%fused_computation.71 | convolution fusion | flops 276040192 | bytes 9969664 | tf_op jit(solution)/shard_map/htk,khd->thd/dot_general | solution.py:199
  366.3 4.7 convolution_bitcast_fusion.1
  376.7 8.7 %fusion.50 = f32[512,8,128]{2,0,1:T(8,128)} fusion(f32[8,256,512]{1,2,0:T(8,128)} %fusion.81, f32[8,256,512]{1,2,0:T(8,128)} %copy-done.16, f32[8,256]{1,0:T(8,128)S(1)} %compare_select_fusion.1, bf16[256,1024]{1,0:T(8,128)(2,1)} %param.32), kind=kOutput, calls=%fused_computation.58 | convolution fusion | flops 275778048 | bytes 11018240 | tf_op jit(solution)/shard_map/htk,thd->khd/dot_general | solution.py:203
  392.3 4.7 pad_maximum_fusion
  397.0 8.4 %reduce-scatter.5.cloned.1.call-start = ((), (), s32[]{:S(2)}) async-start(), calls=%async_computation.9 | async-start | bytes 491520 | tf_op jit(solution)/shard_map/reduce_scatter | solution.py:227
  405.5 9.4 %all-gather.8.cloned.1.call-done = bf16[2048,1024]{0,1:T(8,128)(2,1)} async-done(((bf16[256,1024]{0,1:T(8,128)(2,1)}), bf16[2048,1024]{0,1:T(8,128)(2,1)}) %all-gather.8.cloned.1.call-update) | async-done | bytes 4194320 | tf_op jit(solution)/shard_map/all_gather | solution.py:119
  414.9 15.9 %fusion.4 = (f32[8,256]{1,0:T(8,128)S(1)}, f32[8,2048,256]{1,2,0:T(8,128)}) fusion(f32[8,256]{1,0:T(8,128)S(1)} %get-tuple-element.31, f32[8,256]{1,0:T(8,128)S(1)} %get-tuple-element.36, f32[8,256,2048]{2,1,0:T(8,128)} %copy-done.1, pred[256,2048]{1,0:T(8,128)(4,1)} %fusion.45, bf16[2048,8,128]{0,2,1:T(8,128)(2,1)} %bitcast.210, bf16[256,1024]{1,0:T(8,128)(2,1)} %param.37), kind=kOutput, calls=%fused_computation.7 | convolution fusion | flops 1103099904 | bytes 38821888 | tf_op jit(solution)/shard_map/thd,khd->htk/dot_general | solution.py:143
  430.8 31.9 %all_gather.27 = f32[2048,8]{0,1:T(8,128)S(1)} all-gather(f32[256,8]{0,1:T(8,128)S(1)} %bitcast.207), channel_id=1, replica_groups=mesh['ctx'=8,'vis'=4] {'ctx'}, dimensions={0}, use_global_device_ids=true | all-gather | bytes 73728 | tf_op jit(solution)/shard_map/all_gather | solution.py:164
  462.7 9.7 %fusion.64 = bf16[8,128,256]{2,1,0:T(8,128)(2,1)} fusion(bf16[2048,8,128]{0,2,1:T(8,128)(2,1)S(1)} %bitcast.211, f32[8,256,2048]{2,1,0:T(8,128)} %copy-done.1, f32[8,256]{1,0:T(8,128)S(1)} %get-tuple-element.31, f32[8,256]{1,0:T(8,128)S(1)} %get-tuple-element.36, pred[256,2048]{1,0:T(8,128)(4,1)S(1)} %copy-done.3), kind=kOutput, calls=%fused_computation.68 | convolution fusion | flops 1099169792 | bytes 22036480 | tf_op jit(solution)/shard_map/htk,khd->thd/dot_general | solution.py:139
  472.4 16.3 %fusion.67 = bf16[8,256,128]{1,2,0:T(8,128)(2,1)} fusion(bf16[2048,8,128]{0,2,1:T(8,128)(2,1)} %bitcast.186, f32[8,2048,256]{1,2,0:T(8,128)} %get-tuple-element.39, f32[8,256]{1,0:T(8,128)S(1)} %get-tuple-element.38, f32[8,256,2048]{2,1,0:T(8,128)} %copy-done.1, f32[8,256]{1,0:T(8,128)S(1)} %get-tuple-element.31, f32[8,256]{1,0:T(8,128)S(1)} %get-tuple-element.36, ...), kind=kOutput, calls=%fused_computation.69 | convolution fusion | flops 1111752704 | bytes 38821888 | tf_op jit(solution)/shard_map/htk,khd->thd/dot_general | solution.py:147
  488.7 17.4 %reduce-scatter.3.cloned.1.call-done = f32[1,64,2048]{2,1,0:T(8,128)} async-done(((f32[8,64,2048]{2,1,0:T(8,128)}), f32[1,64,2048]{2,1,0:T(8,128)}) %reduce-scatter.3.cloned.1.call-update) | async-done | bytes 524304 | tf_op jit(solution)/shard_map/reduce_scatter | solution.py:212
  510.2 15.0 %fusion.74 = bf16[8,256,128]{1,2,0:T(8,128)(2,1)} fusion(bf16[2048,8,128]{0,2,1:T(8,128)(2,1)} %bitcast.191, f32[8,2048,256]{2,1,0:T(8,128)} %fusion.84, f32[8,2048]{1,0:T(8,128)S(1)} %bitcast.205, f32[8,2048]{1,0:T(8,128)S(1)} %bitcast.204, pred[2048,256]{1,0:T(8,128)(4,1)} %fusion.46, bf16[256,8,128]{0,2,1:T(8,128)(2,1)} %fusion.70, ...), kind=kOutput, calls=%fused_computation.72 | convolution fusion | flops 2181300224 | bytes 26869760 | tf_op jit(solution)/shard_map/hqk,qhd->khd/dot_general | solution.py:185
  (105 shorter events, 77.1 us)
Async XLA Ops:
  7.2 109.0 %copy-start = (bf16[1536,1024]{1,0:T(8,128)(2,1)S(1)}, bf16[1536,1024]{1,0:T(8,128)(2,1)}, u32[]{:S(2)}) copy-start(bf16[1536,1024]{1,0:T(8,128)(2,1)} %param.27) | copy-start | bytes 9437188
  7.2 56.2 %all-reduce.2.cloned.1.call-start = ((), (), s32[]{:S(2)}) async-start(), calls=%async_computation.2 | async-start | bytes 786432 | tf_op jit(solution)/shard_map/psum | solution.py:90
  9.6 13.3 %copy-start.5 = (bf16[64,1536]{1,0:T(8,128)(2,1)S(1)}, bf16[64,1536]{1,0:T(8,128)(2,1)}, u32[]{:S(2)}) copy-start(bf16[64,1536]{1,0:T(8,128)(2,1)} %param.20) | copy-start | bytes 589828
  9.6 13.3 %copy-start.10 = (f32[1536]{0:T(1024)S(1)}, f32[1536]{0:T(1024)}, u32[]{:S(2)}) copy-start(f32[1536]{0:T(1024)} %param.22) | copy-start | bytes 18436
  25.8 47.9 %copy-start.15 = (f32[8]{0:T(128)S(1)}, f32[8]{0:T(128)}, u32[]{:S(2)}) copy-start(f32[8]{0:T(128)} %param.36) | copy-start | bytes 100
  25.9 47.9 %copy-start.12 = (s32[8]{0:T(128)S(1)}, s32[8]{0:T(128)}, u32[]{:S(2)}) copy-start(s32[8]{0:T(128)} %param.29) | copy-start | bytes 100
  25.9 48.1 %copy-start.9 = (s32[2048]{0:T(1024)S(1)}, s32[2048]{0:T(1024)}, u32[]{:S(2)}) copy-start(s32[2048]{0:T(1024)} %param.30) | copy-start | bytes 24580
  25.9 48.1 %copy-start.11 = (s32[256]{0:T(256)S(1)}, s32[256]{0:T(256)}, u32[]{:S(2)}) copy-start(s32[256]{0:T(256)} %param.31) | copy-start | bytes 3076
  27.9 82.7 %all-gather.6.cloned.1.call-start = ((), (), s32[]{:S(2)}) async-start(), calls=%async_computation.3 | async-start | bytes 1769472 | tf_op jit(solution)/shard_map/all_gather | solution.py:92
  65.1 122.2 %all-gather.10.cloned.1.call-start = ((), (), s32[]{:S(2)}) async-start(), calls=%async_computation.5 | async-start | bytes 4718592 | tf_op jit(solution)/shard_map/all_gather | solution.py:118
  67.2 196.4 %all-gather.12.cloned.1.call-start = ((), (), s32[]{:S(2)}) async-start(), calls=%async_computation.6 | async-start | bytes 4718592 | tf_op jit(solution)/shard_map/all_gather | solution.py:159
  69.4 269.6 %all-gather.14.cloned.1.call-start = ((), (), s32[]{:S(2)}) async-start(), calls=%async_computation.7 | async-start | bytes 4718592 | tf_op jit(solution)/shard_map/all_gather | solution.py:160
  71.5 343.4 %all-gather.8.cloned.1.call-start = ((), (), s32[]{:S(2)}) async-start(), calls=%async_computation.4 | async-start | bytes 4718592 | tf_op jit(solution)/shard_map/all_gather | solution.py:119
  110.6 5.5 %copy-start.14 = (bf16[8,64,1536]{2,1,0:T(8,128)(2,1)S(1)}, bf16[8,64,1536]{2,1,0:T(8,128)(2,1)}, u32[]{:S(2)}) copy-start(bf16[8,64,1536]{2,1,0:T(8,128)(2,1)} %all-gather.6.cloned.1.call-done) | copy-start | bytes 4718596
  123.8 2.2 copy-start.4
  123.8 2.2 copy-start.7
  126.0 2.2 copy-start.16
  128.2 377.8 %reduce-scatter.3.cloned.1.call-start = ((), (), s32[]{:S(2)}) async-start(), calls=%async_computation.8 | async-start | bytes 4718592 | tf_op jit(solution)/shard_map/reduce_scatter | solution.py:212
  187.3 5.5 %copy-start.2 = (pred[256,2048]{1,0:T(8,128)(4,1)S(1)}, pred[256,2048]{1,0:T(8,128)(4,1)}, u32[]{:S(2)}) copy-start(pred[256,2048]{1,0:T(8,128)(4,1)} %fusion.45) | copy-start | bytes 1572868
  192.8 6.1 %copy-start.1 = (f32[8,256,2048]{2,1,0:T(8,128)}, f32[8,256,2048]{2,1,0:T(8,128)S(1)}, u32[]{:S(2)}) copy-start(f32[8,256,2048]{2,1,0:T(8,128)S(1)} %get-tuple-element.37) | copy-start | bytes 50331652
  397.0 134.3 %reduce-scatter.5.cloned.1.call-start = ((), (), s32[]{:S(2)}) async-start(), calls=%async_computation.9 | async-start | bytes 491520 | tf_op jit(solution)/shard_map/reduce_scatter | solution.py:227
  414.9 47.8 %copy-start.3 = (pred[256,2048]{1,0:T(8,128)(4,1)S(1)}, pred[256,2048]{1,0:T(8,128)(4,1)}, u32[]{:S(2)}) copy-start(pred[256,2048]{1,0:T(8,128)(4,1)} %fusion.45) | copy-start | bytes 1572868
  414.9 47.8 %copy-start.13 = (bf16[2048,1024]{0,1:T(8,128)(2,1)S(1)}, bf16[2048,1024]{0,1:T(8,128)(2,1)}, u32[]{:S(2)}) copy-start(bf16[2048,1024]{0,1:T(8,128)(2,1)} %all-gather.8.cloned.1.call-done) | copy-start | bytes 12582916
  506.1 2.3 copy-start.6
  (1 other events, 0.9 us)
Sparse Core Ops, SparseCore 0:
  28.0 35.3 all-reduce.1
  66.4 44.1 all-gather.5
  113.4 73.8 all-gather.9
  189.9 73.6 all-gather.11
  265.7 73.2 all-gather.13
  341.7 73.1 all-gather.7
  419.0 87.0 reduce-scatter.2
  510.4 20.4 reduce-scatter.4
where the time goes:
time: 548 us; the launch traced here: 540 us
  waiting for transfers between devices  253 us (46%)
  matrix products  132 us (24%)
  blocking collectives  62.8 us (11%)
  local copies, waits for them, and re-layouts  41.2 us (8%)
  other arithmetic  27.2 us (5%)
  between operations  14.7 us (3%)
  starting transfers between devices  8.97 us (2%)
    all_gather x1, waiting for transfers between devices, shards(): lax.all_gather(grad_output, 'ctx', axis=0, tiled=True)  64.6 us
    all_gather x1, waiting for transfers between devices, shards(): lax.all_gather(self_key, 'ctx', axis=0, tiled=True)  56 us
    all_gather x1, waiting for transfers between devices, shards(): latent_stack = lax.all_gather(latent_rows, 'ctx', axis=0, tiled=True)  36.4 us
    psum x1, waiting for transfers between devices, shards(): resampled = lax.psum(partial_out, 'vis')  35.4 us
    all_gather x1, waiting for transfers between devices, shards(): lax.all_gather(self_query, 'ctx', axis=0, tiled=True)  33.9 us
    all_gather x1, blocking collectives, shards(): lax.all_gather(row_delta.T, 'ctx', axis=0, tiled=True)  31.9 us
    all_gather x1, blocking collectives, shards(): lax.all_gather(log_total.T, 'ctx', axis=0, tiled=True)  30.8 us
    unnamed x44, local copies, waits for them, and re-layouts  21.1 us
  transfers between devices with their start and end apart: 8, of which 7 were waited for; matrix products, arithmetic and copies ran while one was open for 32% of the time, Pallas kernels for 0%

commit v1 on v0

--- a/solution.py
+++ b/solution.py
@@ -1,8 +1,11 @@
+import functools
 import math
 
 import jax
 import jax.numpy as jnp
 from jax import lax
+from jax.experimental import pallas as pl
+from jax.experimental.pallas import tpu as pltpu
 from jax.sharding import PartitionSpec as P
 
 LATENT_COUNT = 64
@@ -230,6 +233,535 @@
     return (attended, grad_query, grad_key, grad_value, grad_cross_query, grad_latents)
 
 
+F32 = jnp.float32
+BF16 = jnp.bfloat16
+MASKED = -1e30
+
+
+def mm(a, b):
+    return lax.dot_general(a, b, (((1,), (0,)), ((), ())), preferred_element_type=F32)
+
+
+def mm_nt(a, b):
+    return lax.dot_general(a, b, (((1,), (1,)), ((), ())), preferred_element_type=F32)
+
+
+def mm_tn(a, b):
+    return lax.dot_general(a, b, (((0,), (0,)), ((), ())), preferred_element_type=F32)
+
+
+def normed(values, norm_gain):
+    v = values.astype(F32)
+    center = jnp.mean(v, axis=-1, keepdims=True)
+    spread = jnp.mean((v - center) ** 2, axis=-1, keepdims=True)
+    return ((v - center) * lax.rsqrt(spread + 1e-05) * norm_gain).astype(BF16)
+
+
+def head_kernel(
+    nc,
+    nv,
+    feat,
+    lat0,
+    fgain,
+    lgain,
+    wq,
+    wk,
+    wv,
+    wo,
+    xwk,
+    xwv,
+    img_row,
+    seg_row,
+    seg_col,
+    latest,
+    gate,
+    cq_in,
+    q_in,
+    k_in,
+    v_in,
+    g_in,
+    att_out,
+    gq_out,
+    gk_out,
+    gv_out,
+    gcq_out,
+    glat_out,
+    cq,
+    q,
+    k,
+    v,
+    g,
+    wxk,
+    wxv,
+    lat_rows,
+    lat_col,
+    part,
+    part_in,
+    lat_mine,
+    lat_all,
+    xk_loc,
+    xv_loc,
+    xk,
+    xv,
+    vin,
+    cprob,
+    s_buf,
+    dp_buf,
+    dk,
+    dv,
+    att_s,
+    gq_s,
+    gk_s,
+    gv_s,
+    gcq_s,
+    gxk,
+    gxv,
+    gxk_s,
+    gxv_s,
+    own_k,
+    own_v,
+    lpart,
+    lpart_in,
+    w_sem,
+    own_sem,
+    in_send,
+    in_recv,
+    lat_send,
+    lat_recv,
+    p_send,
+    p_recv,
+    l_send,
+    l_recv,
+    x_send,
+    x_recv,
+    o_own,
+    o_send,
+    o_recv,
+    gx_send,
+    gx_recv,
+    r_send,
+    r_recv,
+):
+    me = lax.axis_index("ctx")
+    vi = lax.axis_index("vis")
+    rows = q_in.shape[0]
+    total = rows * nc
+    slots = lat0.shape[0]
+    wide = lat0.shape[1]
+    cut = wide // nv
+    scale = 1.0 / math.sqrt(DH)
+    MESH = pl.DeviceIdType.MESH
+
+    def remote(s, d, ss, rs, c, w):
+        return pltpu.make_async_remote_copy(
+            src_ref=s, dst_ref=d, send_sem=ss, recv_sem=rs, device_id=(c, w), device_id_type=MESH
+        )
+
+    barrier = pltpu.get_barrier_semaphore()
+    for o in range(1, nc):
+        pl.semaphore_signal(barrier, inc=1, device_id=(lax.rem(me + o, nc), vi), device_id_type=MESH)
+    for o in range(1, nv):
+        pl.semaphore_signal(barrier, inc=1, device_id=(me, lax.rem(vi + o, nv)), device_id_type=MESH)
+    pl.semaphore_wait(barrier, nc + nv - 2)
+
+    def head_of(p):
+        return pl.ds(pl.multiple_of(p * DH, DH), DH)
+
+    def rows_of(p):
+        return pl.ds(pl.multiple_of(p * rows, rows), rows)
+
+    def slot_of(p):
+        return pl.ds(pl.multiple_of(p * slots, slots), slots)
+
+    def cut_of(p):
+        return pl.ds(pl.multiple_of(p * cut, cut), cut)
+
+    ins = ((cq_in, cq), (v_in, v), (q_in, q), (k_in, k), (g_in, g))
+
+    def in_copy(a, p):
+        return remote(
+            ins[a][0].at[:, head_of(p)], ins[a][1].at[rows_of(me), :],
+            in_send.at[a, p], in_recv.at[a, me], p, vi,
+        )
+
+    def in_wait(a, p):
+        return remote(
+            ins[a][0].at[:, head_of(p)], ins[a][1].at[rows_of(p), :],
+            in_send.at[a, p], in_recv.at[a, p], p, vi,
+        )
+
+    def lat_copy(p):
+        return remote(latest, lat_rows.at[me], lat_send.at[p], lat_recv.at[me], p, vi)
+
+    def lat_wait(p):
+        return remote(latest, lat_rows.at[p], lat_send.at[p], lat_recv.at[p], p, vi)
+
+    def peers(fn):
+        def step(o, c):
+            fn(lax.rem(me + o, nc))
+            return c
+
+        lax.fori_loop(1, nc, step, 0)
+
+    def mates(fn):
+        for o in range(1, nv):
+            fn(lax.rem(vi + o, nv))
+
+    wcopies = (
+        pltpu.make_async_copy(xwk, wxk, w_sem.at[0]),
+        pltpu.make_async_copy(xwv, wxv, w_sem.at[1]),
+    )
+    for c in wcopies:
+        c.start()
+
+    def start_in(p):
+        lat_copy(p).start()
+        for a in range(5):
+            in_copy(a, p).start()
+
+    peers(start_in)
+    owns = tuple(
+        pltpu.make_async_copy(s.at[:, head_of(me)], d.at[rows_of(me), :], own_sem.at[a])
+        for a, (s, d) in enumerate(ins)
+    )
+    for c in owns:
+        c.start()
+    lat_rows[me] = latest[...]
+
+    f_norm = normed(feat[0], fgain[...])
+    l_norm = normed(lat0[...], lgain[...])
+    rq = mm(l_norm, wq[...]).astype(BF16)
+    rkf = mm(f_norm, wk[...]).astype(BF16)
+    rkl = mm(l_norm, wk[...]).astype(BF16)
+    rvf = mm(f_norm, wv[...]).astype(BF16)
+    rvl = mm(l_norm, wv[...]).astype(BF16)
+    width = rq.shape[1]
+    lane = lax.broadcasted_iota(jnp.int32, (1, width), 1)
+    mix = jnp.zeros((slots, width), F32)
+    r_scale = 1.0 / math.sqrt(RESAMPLER_WIDTH)
+    for h in range(width // RESAMPLER_WIDTH):
+        inside = (lane >= h * RESAMPLER_WIDTH) & (lane < (h + 1) * RESAMPLER_WIDTH)
+        qh = jnp.where(inside, rq, jnp.zeros_like(rq))
+        sf = mm_nt(qh, rkf) * r_scale
+        sl = mm_nt(qh, rkl) * r_scale
+        peak = jnp.maximum(jnp.max(sf, axis=-1, keepdims=True), jnp.max(sl, axis=-1, keepdims=True))
+        ef, el = jnp.exp(sf - peak), jnp.exp(sl - peak)
+        inv = 1.0 / (jnp.sum(ef, axis=-1, keepdims=True) + jnp.sum(el, axis=-1, keepdims=True))
+        mh = mm((ef * inv).astype(BF16), rvf) + mm((el * inv).astype(BF16), rvl)
+        mix = jnp.where(inside, mh, mix)
+    part[...] = mm(mix.astype(BF16), wo[...])
+
+    def p_copy(w):
+        return remote(part.at[:, cut_of(w)], part_in.at[vi], p_send.at[w], p_recv.at[vi], me, w)
+
+    def p_wait(w):
+        return remote(part.at[:, cut_of(w)], part_in.at[w], p_send.at[w], p_recv.at[w], me, w)
+
+    mates(lambda w: p_copy(w).start())
+    part_in[vi] = part[:, cut_of(vi)]
+    mates(lambda w: p_wait(w).wait_recv())
+    summed = part_in[0]
+    for w in range(1, nv):
+        summed = summed + part_in[w]
+    lat_mine[...] = (lat0[:, cut_of(vi)].astype(F32) + summed).astype(BF16)
+
+    def l_copy(w):
+        return remote(lat_mine, lat_all.at[vi], l_send.at[w], l_recv.at[vi], me, w)
+
+    def l_wait(w):
+        return remote(lat_mine, lat_all.at[w], l_send.at[w], l_recv.at[w], me, w)
+
+    mates(lambda w: l_copy(w).start())
+    lat_all[vi] = lat_mine[...]
+    for c in wcopies:
+        c.wait()
+    mates(lambda w: l_wait(w).wait_recv())
+    for wx, loc in ((wxk, xk_loc), (wxv, xv_loc)):
+        acc = mm(lat_all[0], wx[0:cut, :])
+        for w in range(1, nv):
+            acc = acc + mm(lat_all[w], wx[w * cut : (w + 1) * cut, :])
+        loc[...] = acc.astype(BF16)
+
+    xs = ((xk_loc, xk), (xv_loc, xv))
+
+    def x_copy(a, p):
+        return remote(
+            xs[a][0].at[:, head_of(p)], xs[a][1].at[slot_of(me), :],
+            x_send.at[a, p], x_recv.at[a, me], p, vi,
+        )
+
+    def x_wait(a, p):
+        return remote(
+            xs[a][0].at[:, head_of(p)], xs[a][1].at[slot_of(p), :],
+            x_send.at[a, p], x_recv.at[a, p], p, vi,
+        )
+
+    peers(lambda p: (x_copy(0, p).start(), x_copy(1, p).start()))
+    xk[slot_of(me), :] = xk_loc[:, head_of(me)]
+    xv[slot_of(me), :] = xv_loc[:, head_of(me)]
+
+    peers(lambda p: lat_wait(p).wait_recv())
+    for p in range(nc):
+        for c in range(rows // 128):
+            line = lat_rows[p, 0:1, c * 128 : (c + 1) * 128]
+            lat_col[p * rows + c * 128 : p * rows + (c + 1) * 128, :] = jnp.broadcast_to(
+                line, (128, 128)
+            ).T
+
+    peers(lambda p: (x_wait(0, p).wait_recv(), x_wait(1, p).wait_recv()))
+    for c in owns:
+        c.wait()
+
+    def wait_in(p):
+        for a in range(5):
+            in_wait(a, p).wait_recv()
+
+    peers(wait_in)
+
+    images = img_row[0:1, :]
+    gate_h = gate[0:1, 0:1]
+
+    def cross_step(i, carry):
+        r = rows_of(i)
+        allowed = images == lat_col[r, 0:1]
+        s = jnp.where(allowed, mm_nt(cq[r, :], xk[...]) * scale, MASKED)
+        peak = jnp.max(s, axis=-1, keepdims=True)
+        e = jnp.where(allowed, jnp.exp(s - peak), 0.0)
+        tot = jnp.sum(e, axis=-1, keepdims=True)
+        p = e / jnp.where(tot > 0, tot, 1.0)
+        cprob[r, :] = p
+        crossed = mm(p.astype(BF16), xv[...])
+        vin[r, :] = (v[r, :].astype(F32) + gate_h * crossed).astype(BF16)
+        return carry
+
+    lax.fori_loop(0, nc, cross_step, 0)
+
+    dk[...] = jnp.zeros_like(dk)
+    dv[...] = jnp.zeros_like(dv)
+    gxk[...] = jnp.zeros_like(gxk)
+    gxv[...] = jnp.zeros_like(gxv)
+    kc = 2 * rows
+
+    def key_cols(j):
+        return pl.ds(pl.multiple_of(j * kc, kc), kc)
+
+    outs = ((att_s, att_out), (gq_s, gq_out), (gk_s, gk_out), (gv_s, gv_out), (gcq_s, gcq_out))
+
+    def o_copy(a, p):
+        return remote(
+            outs[a][0].at[rows_of(p), :], outs[a][1].at[:, head_of(me)],
+            o_send.at[a, p], o_recv.at[a, me], p, vi,
+        )
+
+    def o_wait(a, p):
+        return remote(
+            outs[a][0].at[rows_of(p), :], outs[a][1].at[:, head_of(p)],
+            o_send.at[a, p], o_recv.at[a, p], p, vi,
+        )
+
+    def o_local(a):
+        return pltpu.make_async_copy(
+            outs[a][0].at[rows_of(me), :], outs[a][1].at[:, head_of(me)], o_own.at[a]
+        )
+
+    def self_step(b, carry):
+        i = nc - 1 - b
+        r = rows_of(i)
+        chunks = i // 2 + 1
+        qi, gi = q[r, :], g[r, :]
+        seg_i = seg_col[r, 0:1]
+        q_pos = i * rows + lax.broadcasted_iota(jnp.int32, (rows, kc), 0)
+        k_iota = lax.broadcasted_iota(jnp.int32, (rows, kc), 1)
+
+        def lanes(x, op):
+            out = x[:, 0:128]
+            for c in range(1, kc // 128):
+                out = op(out, x[:, c * 128 : (c + 1) * 128])
+            return out
+
+        def pass1(j, m):
+            cols = key_cols(j)
+            allowed = (seg_row[0:1, cols] == seg_i) & (j * kc + k_iota <= q_pos)
+            s = jnp.where(allowed, mm_nt(qi, k[cols, :]) * scale, MASKED)
+            s_buf[:, cols] = s
+            return jnp.maximum(m, lanes(s, jnp.maximum))
+
+        m = lax.fori_loop(0, chunks, pass1, jnp.full((rows, 128), MASKED, F32))
+        m = jnp.max(m, axis=-1, keepdims=True)
+
+        def pass2(j, c):
+            tot, dl, acc = c
+            cols = key_cols(j)
+            p = jnp.exp(s_buf[:, cols] - m)
+            s_buf[:, cols] = p
+            vj = vin[cols, :]
+            dp = mm_nt(gi, vj)
+            dp_buf[:, cols] = dp
+            return tot + lanes(p, jnp.add), dl + lanes(p * dp, jnp.add), acc + mm(p.astype(BF16), vj)
+
+        zero = jnp.zeros((rows, 128), F32)
+        tot, dl, acc = lax.fori_loop(0, chunks, pass2, (zero, zero, zero))
+        inv = 1.0 / jnp.sum(tot, axis=-1, keepdims=True)
+        delta = jnp.sum(dl, axis=-1, keepdims=True) * inv
+        att_s[r, :] = (acc * inv).astype(BF16)
+
+        def pass3(j, acc):
+            cols = key_cols(j)
+            p = s_buf[:, cols] * inv
+            ds = (p * (dp_buf[:, cols] - delta) * scale).astype(BF16)
+            dk[cols, :] += mm_tn(ds, qi)
+            dv[cols, :] += mm_tn(p.astype(BF16), gi)
+            return acc + mm(ds, k[cols, :])
+
+        gq_s[r, :] = lax.fori_loop(0, chunks, pass3, zero).astype(BF16)
+        dvi = dv[r, :]
+        gk_s[r, :] = dk[r, :].astype(BF16)
+        gv_s[r, :] = dvi.astype(BF16)
+
+        dc = (gate_h * dvi).astype(BF16)
+        cp = cprob[r, :]
+        cd = mm_nt(dc, xv[...])
+        cs = (cp * (cd - jnp.sum(cp * cd, axis=-1, keepdims=True)) * scale).astype(BF16)
+        gcq_s[r, :] = mm(cs, xk[...]).astype(BF16)
+        gxk[...] += mm_tn(cs, cq[r, :])
+        gxv[...] += mm_tn(cp.astype(BF16), dc)
+
+        @pl.when(i != me)
+        def _():
+            for a in range(5):
+                o_copy(a, i).start()
+
+        @pl.when(i == me)
+        def _():
+            for a in range(5):
+                o_local(a).start()
+
+        return carry
+
+    lax.fori_loop(0, nc, self_step, 0)
+
+    gxk_s[...] = gxk[...].astype(BF16)
+    gxv_s[...] = gxv[...].astype(BF16)
+    gxs = ((gxk_s, own_k), (gxv_s, own_v))
+
+    def gx_copy(a, p):
+        return remote(
+            gxs[a][0].at[slot_of(p), :], gxs[a][1].at[:, head_of(me)],
+            gx_send.at[a, p], gx_recv.at[a, me], p, vi,
+        )
+
+    def gx_wait(a, p):
+        return remote(
+            gxs[a][0].at[slot_of(p), :], gxs[a][1].at[:, head_of(p)],
+            gx_send.at[a, p], gx_recv.at[a, p], p, vi,
+        )
+
+    peers(lambda p: (gx_copy(0, p).start(), gx_copy(1, p).start()))
+    own_k[:, head_of(me)] = gxk_s[slot_of(me), :]
+    own_v[:, head_of(me)] = gxv_s[slot_of(me), :]
+    peers(lambda p: (gx_wait(0, p).wait_recv(), gx_wait(1, p).wait_recv()))
+    lpart[...] = mm_nt(own_k[...], wxk[...]) + mm_nt(own_v[...], wxv[...])
+
+    def r_copy(w):
+        return remote(lpart.at[:, cut_of(w)], lpart_in.at[vi], r_send.at[w], r_recv.at[vi], me, w)
+
+    def r_wait(w):
+        return remote(lpart.at[:, cut_of(w)], lpart_in.at[w], r_send.at[w], r_recv.at[w], me, w)
+
+    mates(lambda w: r_copy(w).start())
+    lpart_in[vi] = lpart[:, cut_of(vi)]
+    mates(lambda w: r_wait(w).wait_recv())
+    summed = lpart_in[0]
+    for w in range(1, nv):
+        summed = summed + lpart_in[w]
+    glat_out[0] = summed.astype(BF16)
+
+    def finish(p):
+        lat_wait(p).wait_send()
+        for a in range(5):
+            in_wait(a, p).wait_send()
+            o_wait(a, p).wait()
+        for a in range(2):
+            x_wait(a, p).wait_send()
+            gx_wait(a, p).wait_send()
+
+    peers(finish)
+
+    def finish_mate(w):
+        p_wait(w).wait_send()
+        l_wait(w).wait_send()
+        r_wait(w).wait_send()
+
+    mates(finish_mate)
+    for a in range(5):
+        o_local(a).wait()
+
+
+def by_head(nc, nv, *args):
+    (feat, lat0, fgain, lgain, wq, wk, wv, wo, xwk, xwv, slot_image, segments, latest_image,
+     cross_query, self_query, self_key, self_value, cross_gate, grad_output) = args
+    rows, cols = self_query.shape
+    total = rows * nc
+    slots, wide = lat0.shape
+    xrows = nc * slots
+    cut = wide // nv
+    gate = jnp.tanh(lax.dynamic_slice_in_dim(cross_gate, lax.axis_index("ctx"), 1, 0))
+    gate = jnp.broadcast_to(gate[None], (8, 128))
+    img_row = jnp.broadcast_to(jnp.repeat(slot_image, slots).astype(F32)[None], (8, xrows))
+    seg_row = jnp.broadcast_to(segments[None], (8, total))
+    seg_col = jnp.broadcast_to(segments[:, None], (total, 128))
+    latest = jnp.broadcast_to(latest_image.astype(F32)[None], (8, rows))
+    vmem = pl.BlockSpec(memory_space=pltpu.VMEM)
+    hbm = pl.BlockSpec(memory_space=pl.ANY)
+    tok = jax.ShapeDtypeStruct((rows, cols), BF16)
+    V = pltpu.VMEM
+    dma = pltpu.SemaphoreType.DMA
+    scratch = (
+        [V((total, DH), BF16)] * 5
+        + [V((wide, cols), BF16)] * 2
+        + [V((nc, 8, rows), F32), V((total, 128), F32)]
+        + [V((slots, wide), F32), V((nv, slots, cut), F32)]
+        + [V((slots, cut), BF16), V((nv, slots, cut), BF16)]
+        + [V((slots, cols), BF16)] * 2
+        + [V((xrows, DH), BF16)] * 2
+        + [V((total, DH), BF16), V((total, xrows), F32)]
+        + [V((rows, total), F32)] * 2
+        + [V((total, DH), F32)] * 2
+        + [V((total, DH), BF16)] * 5
+        + [V((xrows, DH), F32)] * 2
+        + [V((xrows, DH), BF16)] * 2
+        + [V((slots, cols), BF16)] * 2
+        + [V((slots, wide), F32), V((nv, slots, cut), F32)]
+        + [dma((2,)), dma((5,))]
+        + [dma((5, nc))] * 2
+        + [dma((nc,))] * 2
+        + [dma((nv,))] * 4
+        + [dma((2, nc))] * 2
+        + [dma((5,))]
+        + [dma((5, nc))] * 2
+        + [dma((2, nc))] * 2
+        + [dma((nv,))] * 2
+    )
+    return pl.pallas_call(
+        functools.partial(head_kernel, nc, nv),
+        out_shape=[tok] * 5 + [jax.ShapeDtypeStruct((1, slots, cut), BF16)],
+        in_specs=[vmem] * 8 + [hbm] * 2 + [vmem] * 5 + [hbm] * 5,
+        out_specs=[hbm] * 5 + [vmem],
+        scratch_shapes=scratch,
+        compiler_params=pltpu.CompilerParams(
+            collective_id=0, has_side_effects=True, vmem_limit_bytes=52 * 1024 * 1024
+        ),
+        name="head_window",
+    )(feat, lat0, fgain[None], lgain[None], wq, wk, wv, wo, xwk, xwv, img_row, seg_row, seg_col,
+      latest, gate, cross_query, self_query, self_key, self_value, grad_output)
+
+
+def dispatch(nc, nv, *args):
+    if args[17].shape[0] == nc and args[0].shape[0] == 1:
+        return tuple(by_head(nc, nv, *args))
+    return shards(*args)
+
+
 def solution(mesh):
     in_specs = (
         P("ctx", None, None),
@@ -260,4 +792,5 @@
         P("ctx", "vis"),
         P("ctx", None, "vis"),
     )
-    return jax.shard_map(shards, mesh=mesh, in_specs=in_specs, out_specs=out_specs, check_vma=False)
+    body = functools.partial(dispatch, mesh.shape["ctx"], mesh.shape["vis"])
+    return jax.shard_map(body, mesh=mesh, in_specs=in_specs, out_specs=out_specs, check_vma=False)

time: 548 us -> 191 us (0.35); the launches traced: 540 us -> 190 us
  waiting for transfers between devices: 253 us -> 0 us
  Pallas kernels: 0 us -> 169 us
  matrix products: 132 us -> 0 us
  blocking collectives: 62.8 us -> 0 us
  other arithmetic: 27.2 us -> 1.34 us
  local copies, waits for them, and re-layouts: 41.2 us -> 18.3 us
  between operations: 14.7 us -> 1.37 us
  starting transfers between devices: 8.97 us -> 0 us
    all_gather x5 -> x0, waiting for transfers between devices: 200 us -> none  [the longest x1 64.6 us: shards(): lax.all_gather(grad_output, 'ctx', axis=0, tiled=True)]
    pallas_call x0 -> x1, Pallas kernels: none -> 169 us  [by_head(): pl.pallas_call(functools.partial(head_kernel, nc, nv), out_shape=[tok] *...]
    dot_general x23 -> x0, matrix products: 132 us -> none  [the longest x1 16.3 us: shards(): jnp.einsum('htk,khd->thd', d_score, keys_all, preferred_element_type=sing...]
    all_gather x2 -> x0, blocking collectives: 62.8 us -> none  [the longest x1 31.9 us: shards(): lax.all_gather(row_delta.T, 'ctx', axis=0, tiled=True)]
    psum x1 -> x0, waiting for transfers between devices: 35.4 us -> none  [shards(): resampled = lax.psum(partial_out, 'vis')]
    reduce_scatter x2 -> x0, waiting for transfers between devices: 17.4 us -> none  [the longest x1 17.4 us: shards(): lax.psum_scatter(stacked, 'ctx', scatter_dimension=0, tiled=True)]
    reduce_sum x6 -> x0, other arithmetic: 10.4 us -> none  [the longest x1 5.03 us: masked_softmax(): summed = jnp.sum(raised, axis=-1, keepdims=True)]
    reduce_scatter x2 -> x0, starting transfers between devices: 8.72 us -> none  [the longest x1 8.42 us: shards(): lax.psum_scatter(latent_part, 'vis', scatter_dimension=2, tiled=True)]
  transfers between devices with their start and end apart: 8 -> 0, of which waited for: 7 -> 0; matrix products, arithmetic and copies ran while one was open for 32% -> 0% of each run, Pallas kernels for 0% -> 0%
where the time goes in v1:
time: 191 us; the launch traced here: 190 us
  Pallas kernels  169 us (88%)
  local copies, waits for them, and re-layouts  18.3 us (10%)
    pallas_call x1, Pallas kernels, by_head(): pl.pallas_call(functools.partial(head_kernel, nc, nv), out_shape=[tok] *...  169 us
    unnamed x20, local copies, waits for them, and re-layouts  12.8 us

profile of v1, /device:TPU:0, one launch (start us, length us, event | category | flops | bytes accessed | tf_op | source)
XLA Modules:
  0.0 189.9 jit_solution(7773040538367690469)
XLA Ops:
  0.6 1.2 dynamic_slice.3
  2.6 0.7 convert_element_type.14
  3.2 0.7 convert_element_type.16
  3.9 0.1 broadcast_in_dim.20
  4.0 0.1 convert_element_type.15
  4.1 0.7 broadcast_in_dim.18.fgain
  4.8 0.7 broadcast_in_dim.19.lgain
  5.5 0.7 broadcast_in_dim.22.seg_row
  6.2 2.0 %broadcast_in_dim.46.seg_col = s32[2048,128]{1,0:T(8,128)} broadcast(s32[2048]{0:T(1024)} %param.30), dimensions={0} | broadcast | bytes 1056768 | tf_op jit(solution)/shard_map/broadcast_in_dim | solution.py:712
  8.2 1.0 copy-done
  9.2 1.0 copy-done.1
  10.2 1.0 copy-done.2
  11.2 1.0 copy-done.3
  12.2 0.9 copy-done.4
  13.1 168.8 %head_window.1 = (bf16[256,1024]{1,0:T(8,128)(2,1)}, bf16[256,1024]{1,0:T(8,128)(2,1)}, bf16[256,1024]{1,0:T(8,128)(2,1)}, bf16[256,1024]{1,0:T(8,128)(2,1)}, bf...) custom-call(bf16[1,256,1536]{2,1,0:T(8,128)(2,1)} %feat.1, bf16[64,1536]{1,0:T(8,128)(2,1)S(1)} %copy-done.4, ...), custom_call_target="tpu_custom_call" | custom-call | tf_op jit(solution)/shard_map/head_window/pallas_call | solution.py:745
  181.9 0.0 copy-start.6
  181.9 0.0 copy-start.5
  181.9 2.0 %copy.31 = bf16[256,1024]{1,0:T(8,128)(2,1)} copy(bf16[256,1024]{1,0:T(8,128)(2,1)} %get-tuple-element.12) | data formatting | bytes 1048576
  183.9 1.9 copy.32
  185.8 1.9 copy.33
  187.6 0.0 copy-done.6
  187.6 0.8 copy.34
  188.4 0.8 copy.35
  189.2 0.6 copy.36
  (9 shorter events, 0.0 us)
Async XLA Ops:
  8.2 1.0 copy-start
  9.2 1.0 copy-start.1
  10.2 1.0 copy-start.2
  11.2 1.0 copy-start.3
  12.2 0.9 copy-start.4
  181.9 5.7 %copy-start.6 = (bf16[256,1024]{1,0:T(8,128)(2,1)S(1)}, bf16[256,1024]{1,0:T(8,128)(2,1)}, u32[]{:S(2)}) copy-start(bf16[256,1024]{1,0:T(8,128)(2,1)} %get-tuple-element.15) | copy-start | bytes 1572868
  181.9 6.5 %copy-start.5 = (bf16[256,1024]{1,0:T(8,128)(2,1)S(1)}, bf16[256,1024]{1,0:T(8,128)(2,1)}, u32[]{:S(2)}) copy-start(bf16[256,1024]{1,0:T(8,128)(2,1)} %get-tuple-element.16) | copy-start | bytes 1572868

commit v2 on v1

--- a/solution.py
+++ b/solution.py
@@ -260,21 +260,20 @@
 def head_kernel(
     nc,
     nv,
-    feat,
-    lat0,
-    fgain,
-    lgain,
-    wq,
-    wk,
-    wv,
-    wo,
+    feat_in,
+    lat0_in,
+    fgain_in,
+    lgain_in,
+    wq_in,
+    wk_in,
+    wv_in,
+    wo_in,
     xwk,
     xwv,
-    img_row,
-    seg_row,
-    seg_col,
+    slot_hbm,
+    seg_hbm,
     latest,
-    gate,
+    gate_hbm,
     cq_in,
     q_in,
     k_in,
@@ -286,6 +285,17 @@
     gv_out,
     gcq_out,
     glat_out,
+    feat,
+    lat0,
+    fgain,
+    lgain,
+    wq,
+    wk,
+    wv,
+    wo,
+    slot_in,
+    seg_row,
+    gate,
     cq,
     q,
     k,
@@ -295,6 +305,7 @@
     wxv,
     lat_rows,
     lat_col,
+    seg_col,
     part,
     part_in,
     lat_mine,
@@ -306,7 +317,8 @@
     vin,
     cprob,
     s_buf,
-    dp_buf,
+    inv_s,
+    o_s,
     dk,
     dv,
     att_s,
@@ -346,8 +358,8 @@
     vi = lax.axis_index("vis")
     rows = q_in.shape[0]
     total = rows * nc
-    slots = lat0.shape[0]
-    wide = lat0.shape[1]
+    slots = lat0_in.shape[0]
+    wide = lat0_in.shape[1]
     cut = wide // nv
     scale = 1.0 / math.sqrt(DH)
     MESH = pl.DeviceIdType.MESH
@@ -357,6 +369,20 @@
             src_ref=s, dst_ref=d, send_sem=ss, recv_sem=rs, device_id=(c, w), device_id_type=MESH
         )
 
+    small = (
+        (feat_in, feat), (lat0_in, lat0), (fgain_in, fgain), (lgain_in, lgain),
+        (wq_in, wq), (wk_in, wk), (wv_in, wv), (wo_in, wo),
+        (slot_hbm, slot_in), (seg_hbm, seg_row), (gate_hbm, gate), (latest, lat_rows.at[me]),
+    )
+    smalls = tuple(
+        pltpu.make_async_copy(s, d, w_sem.at[2 + a]) for a, (s, d) in enumerate(small)
+    )
+    wcopies = (
+        pltpu.make_async_copy(xwk, wxk, w_sem.at[0]),
+        pltpu.make_async_copy(xwv, wxv, w_sem.at[1]),
+    )
+    for c in smalls:
+        c.start()
     barrier = pltpu.get_barrier_semaphore()
     for o in range(1, nc):
         pl.semaphore_signal(barrier, inc=1, device_id=(lax.rem(me + o, nc), vi), device_id_type=MESH)
@@ -376,7 +402,7 @@
     def cut_of(p):
         return pl.ds(pl.multiple_of(p * cut, cut), cut)
 
-    ins = ((cq_in, cq), (v_in, v), (q_in, q), (k_in, k), (g_in, g))
+    ins = ((q_in, q), (k_in, k), (cq_in, cq), (v_in, v), (g_in, g))
 
     def in_copy(a, p):
         return remote(
@@ -407,27 +433,20 @@
         for o in range(1, nv):
             fn(lax.rem(vi + o, nv))
 
-    wcopies = (
-        pltpu.make_async_copy(xwk, wxk, w_sem.at[0]),
-        pltpu.make_async_copy(xwv, wxv, w_sem.at[1]),
-    )
+    peers(lambda p: lat_copy(p).start())
+    for a in range(5):
+        peers(lambda p: in_copy(a, p).start())
     for c in wcopies:
         c.start()
-
-    def start_in(p):
-        lat_copy(p).start()
-        for a in range(5):
-            in_copy(a, p).start()
-
-    peers(start_in)
     owns = tuple(
         pltpu.make_async_copy(s.at[:, head_of(me)], d.at[rows_of(me), :], own_sem.at[a])
         for a, (s, d) in enumerate(ins)
     )
     for c in owns:
         c.start()
-    lat_rows[me] = latest[...]
-
+
+    for c in smalls:
+        c.wait()
     f_norm = normed(feat[0], fgain[...])
     l_norm = normed(lat0[...], lgain[...])
     rq = mm(l_norm, wq[...]).astype(BF16)
@@ -500,26 +519,78 @@
     xk[slot_of(me), :] = xk_loc[:, head_of(me)]
     xv[slot_of(me), :] = xv_loc[:, head_of(me)]
 
+    def turned(line):
+        return jnp.broadcast_to(line.astype(F32), (128, 128)).T
+
+    for c in range(total // 128):
+        seg_col[c * 128 : (c + 1) * 128, :] = turned(seg_row[0:1, c * 128 : (c + 1) * 128])
+    kc = 2 * rows
+
+    def key_cols(j):
+        return pl.ds(pl.multiple_of(j * kc, kc), kc)
+
+    def wait_in(a):
+        owns[a].wait()
+        peers(lambda p: in_wait(a, p).wait_recv())
+
+    wait_in(0)
+    wait_in(1)
+
+    def lanes(x, op):
+        out = x[:, 0:128]
+        for c in range(1, kc // 128):
+            out = op(out, x[:, c * 128 : (c + 1) * 128])
+        return out
+
+    zero = jnp.zeros((rows, 128), F32)
+
+    def soft_step(i, carry):
+        r = rows_of(i)
+        chunks = i // 2 + 1
+        qi = q[r, :]
+        seg_i = seg_col[r, 0:1]
+        q_pos = i * rows + lax.broadcasted_iota(jnp.int32, (rows, kc), 0)
+        k_iota = lax.broadcasted_iota(jnp.int32, (rows, kc), 1)
+
+        def pass1(j, m):
+            cols = key_cols(j)
+            allowed = (seg_row[0:1, cols].astype(F32) == seg_i) & (j * kc + k_iota <= q_pos)
+            s = jnp.where(allowed, mm_nt(qi, k[cols, :]) * scale, MASKED)
+            s_buf[r, cols] = s
+            return jnp.maximum(m, lanes(s, jnp.maximum))
+
+        m = lax.fori_loop(0, chunks, pass1, jnp.full((rows, 128), MASKED, F32))
+        m = jnp.max(m, axis=-1, keepdims=True)
+
+        def pass2(j, tot):
+            cols = key_cols(j)
+            p = jnp.exp(s_buf[r, cols] - m)
+            s_buf[r, cols] = p
+            return tot + lanes(p, jnp.add)
+
+        tot = lax.fori_loop(0, chunks, pass2, zero)
+        inv_s[r, :] = jnp.broadcast_to(1.0 / jnp.sum(tot, axis=-1, keepdims=True), (rows, 128))
+        return carry
+
+    lax.fori_loop(0, nc, soft_step, 0)
+
     peers(lambda p: lat_wait(p).wait_recv())
     for p in range(nc):
         for c in range(rows // 128):
-            line = lat_rows[p, 0:1, c * 128 : (c + 1) * 128]
-            lat_col[p * rows + c * 128 : p * rows + (c + 1) * 128, :] = jnp.broadcast_to(
-                line, (128, 128)
-            ).T
-
+            lat_col[p * rows + c * 128 : p * rows + (c + 1) * 128, :] = turned(
+                lat_rows[p, 0:1, c * 128 : (c + 1) * 128]
+            )
     peers(lambda p: (x_wait(0, p).wait_recv(), x_wait(1, p).wait_recv()))
-    for c in owns:
-        c.wait()
-
-    def wait_in(p):
-        for a in range(5):
-            in_wait(a, p).wait_recv()
-
-    peers(wait_in)
-
-    images = img_row[0:1, :]
-    gate_h = gate[0:1, 0:1]
+    slot_of_key = lax.broadcasted_iota(jnp.int32, (1, nc * slots), 1) // slots
+    images = jnp.zeros((1, nc * slots), F32)
+    for p in range(nc):
+        images = jnp.where(slot_of_key == p, slot_in[0:1, p : p + 1].astype(F32), images)
+    gate_lane = lax.broadcasted_iota(jnp.int32, gate.shape, 1)
+    gate_h = jnp.tanh(
+        jnp.sum(jnp.where(gate_lane == me, gate[...], 0.0), axis=-1, keepdims=True)
+    )
+    wait_in(2)
+    wait_in(3)
 
     def cross_step(i, carry):
         r = rows_of(i)
@@ -540,11 +611,6 @@
     dv[...] = jnp.zeros_like(dv)
     gxk[...] = jnp.zeros_like(gxk)
     gxv[...] = jnp.zeros_like(gxv)
-    kc = 2 * rows
-
-    def key_cols(j):
-        return pl.ds(pl.multiple_of(j * kc, kc), kc)
-
     outs = ((att_s, att_out), (gq_s, gq_out), (gk_s, gk_out), (gv_s, gv_out), (gcq_s, gcq_out))
 
     def o_copy(a, p):
@@ -563,59 +629,52 @@
         return pltpu.make_async_copy(
             outs[a][0].at[rows_of(me), :], outs[a][1].at[:, head_of(me)], o_own.at[a]
         )
+
+    def send(a, i):
+        @pl.when(i != me)
+        def _():
+            o_copy(a, i).start()
+
+        @pl.when(i == me)
+        def _():
+            o_local(a).start()
+
+    def att_step(b, carry):
+        i = lax.rem(me + 1 + b, nc)
+        r = rows_of(i)
+
+        def pass_o(j, acc):
+            cols = key_cols(j)
+            return acc + mm(s_buf[r, cols].astype(BF16), vin[cols, :])
+
+        o = lax.fori_loop(0, i // 2 + 1, pass_o, zero) * inv_s[r, 0:1]
+        o_s[r, :] = o
+        att_s[r, :] = o.astype(BF16)
+        send(0, i)
+        return carry
+
+    lax.fori_loop(0, nc, att_step, 0)
+    wait_in(4)
 
     def self_step(b, carry):
         i = nc - 1 - b
         r = rows_of(i)
         chunks = i // 2 + 1
         qi, gi = q[r, :], g[r, :]
-        seg_i = seg_col[r, 0:1]
-        q_pos = i * rows + lax.broadcasted_iota(jnp.int32, (rows, kc), 0)
-        k_iota = lax.broadcasted_iota(jnp.int32, (rows, kc), 1)
-
-        def lanes(x, op):
-            out = x[:, 0:128]
-            for c in range(1, kc // 128):
-                out = op(out, x[:, c * 128 : (c + 1) * 128])
-            return out
-
-        def pass1(j, m):
-            cols = key_cols(j)
-            allowed = (seg_row[0:1, cols] == seg_i) & (j * kc + k_iota <= q_pos)
-            s = jnp.where(allowed, mm_nt(qi, k[cols, :]) * scale, MASKED)
-            s_buf[:, cols] = s
-            return jnp.maximum(m, lanes(s, jnp.maximum))
-
-        m = lax.fori_loop(0, chunks, pass1, jnp.full((rows, 128), MASKED, F32))
-        m = jnp.max(m, axis=-1, keepdims=True)
-
-        def pass2(j, c):
-            tot, dl, acc = c
-            cols = key_cols(j)
-            p = jnp.exp(s_buf[:, cols] - m)
-            s_buf[:, cols] = p
-            vj = vin[cols, :]
-            dp = mm_nt(gi, vj)
-            dp_buf[:, cols] = dp
-            return tot + lanes(p, jnp.add), dl + lanes(p * dp, jnp.add), acc + mm(p.astype(BF16), vj)
-
-        zero = jnp.zeros((rows, 128), F32)
-        tot, dl, acc = lax.fori_loop(0, chunks, pass2, (zero, zero, zero))
-        inv = 1.0 / jnp.sum(tot, axis=-1, keepdims=True)
-        delta = jnp.sum(dl, axis=-1, keepdims=True) * inv
-        att_s[r, :] = (acc * inv).astype(BF16)
+        inv = inv_s[r, 0:1]
+        delta = jnp.sum(o_s[r, :] * gi.astype(F32), axis=-1, keepdims=True)
 
         def pass3(j, acc):
             cols = key_cols(j)
-            p = s_buf[:, cols] * inv
-            ds = (p * (dp_buf[:, cols] - delta) * scale).astype(BF16)
+            p = s_buf[r, cols] * inv
+            ds = (p * (mm_nt(gi, vin[cols, :]) - delta)).astype(BF16)
             dk[cols, :] += mm_tn(ds, qi)
             dv[cols, :] += mm_tn(p.astype(BF16), gi)
             return acc + mm(ds, k[cols, :])
 
-        gq_s[r, :] = lax.fori_loop(0, chunks, pass3, zero).astype(BF16)
+        gq_s[r, :] = (lax.fori_loop(0, chunks, pass3, zero) * scale).astype(BF16)
         dvi = dv[r, :]
-        gk_s[r, :] = dk[r, :].astype(BF16)
+        gk_s[r, :] = (dk[r, :] * scale).astype(BF16)
         gv_s[r, :] = dvi.astype(BF16)
 
         dc = (gate_h * dvi).astype(BF16)
@@ -626,16 +685,8 @@
         gxk[...] += mm_tn(cs, cq[r, :])
         gxv[...] += mm_tn(cp.astype(BF16), dc)
 
-        @pl.when(i != me)
-        def _():
-            for a in range(5):
-                o_copy(a, i).start()
-
-        @pl.when(i == me)
-        def _():
-            for a in range(5):
-                o_local(a).start()
-
+        send(3, i)
+        send(4, i)
         return carry
 
     lax.fori_loop(0, nc, self_step, 0)
@@ -657,6 +708,9 @@
         )
 
     peers(lambda p: (gx_copy(0, p).start(), gx_copy(1, p).start()))
+    send_o = lambda a: (o_local(a).start(), peers(lambda p: o_copy(a, p).start()))
+    send_o(1)
+    send_o(2)
     own_k[:, head_of(me)] = gxk_s[slot_of(me), :]
     own_v[:, head_of(me)] = gxv_s[slot_of(me), :]
     peers(lambda p: (gx_wait(0, p).wait_recv(), gx_wait(1, p).wait_recv()))
@@ -705,34 +759,33 @@
     slots, wide = lat0.shape
     xrows = nc * slots
     cut = wide // nv
-    gate = jnp.tanh(lax.dynamic_slice_in_dim(cross_gate, lax.axis_index("ctx"), 1, 0))
-    gate = jnp.broadcast_to(gate[None], (8, 128))
-    img_row = jnp.broadcast_to(jnp.repeat(slot_image, slots).astype(F32)[None], (8, xrows))
-    seg_row = jnp.broadcast_to(segments[None], (8, total))
-    seg_col = jnp.broadcast_to(segments[:, None], (total, 128))
-    latest = jnp.broadcast_to(latest_image.astype(F32)[None], (8, rows))
     vmem = pl.BlockSpec(memory_space=pltpu.VMEM)
-    hbm = pl.BlockSpec(memory_space=pl.ANY)
+    hbm = pl.BlockSpec(memory_space=pltpu.HBM)
     tok = jax.ShapeDtypeStruct((rows, cols), BF16)
     V = pltpu.VMEM
     dma = pltpu.SemaphoreType.DMA
     scratch = (
-        [V((total, DH), BF16)] * 5
+        [V((1,) + feat.shape[1:], BF16), V((slots, wide), BF16)]
+        + [V((1, wide), F32)] * 2
+        + [V(wq.shape, BF16)] * 3
+        + [V(wo.shape, BF16)]
+        + [V((1, nc), jnp.int32), V((1, total), jnp.int32), V((1, nc), F32)]
+        + [V((total, DH), BF16)] * 5
         + [V((wide, cols), BF16)] * 2
-        + [V((nc, 8, rows), F32), V((total, 128), F32)]
+        + [V((nc, 1, rows), jnp.int32)] + [V((total, 128), F32)] * 2
         + [V((slots, wide), F32), V((nv, slots, cut), F32)]
         + [V((slots, cut), BF16), V((nv, slots, cut), BF16)]
         + [V((slots, cols), BF16)] * 2
         + [V((xrows, DH), BF16)] * 2
         + [V((total, DH), BF16), V((total, xrows), F32)]
-        + [V((rows, total), F32)] * 2
+        + [V((total, total), F32)] + [V((total, DH), F32)] * 2
         + [V((total, DH), F32)] * 2
         + [V((total, DH), BF16)] * 5
         + [V((xrows, DH), F32)] * 2
         + [V((xrows, DH), BF16)] * 2
         + [V((slots, cols), BF16)] * 2
         + [V((slots, wide), F32), V((nv, slots, cut), F32)]
-        + [dma((2,)), dma((5,))]
+        + [dma((14,)), dma((5,))]
         + [dma((5, nc))] * 2
         + [dma((nc,))] * 2
         + [dma((nv,))] * 4
@@ -742,18 +795,41 @@
         + [dma((2, nc))] * 2
         + [dma((nv,))] * 2
     )
-    return pl.pallas_call(
+    got = pl.pallas_call(
         functools.partial(head_kernel, nc, nv),
         out_shape=[tok] * 5 + [jax.ShapeDtypeStruct((1, slots, cut), BF16)],
-        in_specs=[vmem] * 8 + [hbm] * 2 + [vmem] * 5 + [hbm] * 5,
+        in_specs=[hbm] * 19,
         out_specs=[hbm] * 5 + [vmem],
         scratch_shapes=scratch,
         compiler_params=pltpu.CompilerParams(
-            collective_id=0, has_side_effects=True, vmem_limit_bytes=52 * 1024 * 1024
+            collective_id=0, has_side_effects=True, vmem_limit_bytes=62 * 1024 * 1024
         ),
         name="head_window",
-    )(feat, lat0, fgain[None], lgain[None], wq, wk, wv, wo, xwk, xwv, img_row, seg_row, seg_col,
-      latest, gate, cross_query, self_query, self_key, self_value, grad_output)
+    )(feat, lat0, fgain[None], lgain[None], wq, wk, wv, wo, xwk, xwv, slot_image[None],
+      segments[None], latest_image[None], cross_gate[None], cross_query, self_query, self_key,
+      self_value, grad_output)
+    moved = pl.pallas_call(
+        copy_kernel,
+        out_shape=[tok] * 5,
+        in_specs=[hbm] * 5,
+        out_specs=[hbm] * 5,
+        scratch_shapes=[V(tok.shape, BF16)] * 5 + [dma((2, 5))],
+        name="results",
+    )(*got[:5])
+    return (*moved, got[5])
+
+
+def copy_kernel(*refs):
+    src, dst, held, sem = refs[:5], refs[5:10], refs[10:15], refs[15]
+    first = [pltpu.make_async_copy(src[a], held[a], sem.at[0, a]) for a in range(5)]
+    second = [pltpu.make_async_copy(held[a], dst[a], sem.at[1, a]) for a in range(5)]
+    for c in first:
+        c.start()
+    for a in range(5):
+        first[a].wait()
+        second[a].start()
+    for c in second:
+        c.wait()
 
 
 def dispatch(nc, nv, *args):

time: 191 us -> 155 us (0.81)
  Pallas kernels: 169 us -> 150 us
  local copies, waits for them, and re-layouts: 18.3 us -> 4.01 us
    pallas_call x1, Pallas kernels: 169 us -> 147 us  [by_head(): pl.pallas_call(functools.partial(head_kernel, nc, nv), out_shape=[tok] *...]
    unnamed x20 -> x1, local copies, waits for them, and re-layouts: 12.8 us -> 1.42 us
    broadcast_in_dim x6 -> x0, local copies, waits for them, and re-layouts: 2.78 us -> none  [the longest x1 2 us: by_head(): seg_col = jnp.broadcast_to(segments[:, None], (total, 128))]
    pallas_call x0 -> x1, Pallas kernels: none -> 2.61 us  [by_head(): pl.pallas_call(copy_kernel, out_shape=[tok] * 5, in_specs=[hbm] * 5, out_...]
where the time goes in v2:
time: 155 us; the launch traced here: 154 us
  Pallas kernels  150 us (97%)
  local copies, waits for them, and re-layouts  4.01 us (3%)
    pallas_call x1, Pallas kernels, by_head(): pl.pallas_call(functools.partial(head_kernel, nc, nv), out_shape=[tok] *...  147 us

profile of v2, /device:TPU:0, one launch (start us, length us, event | category | flops | bytes accessed | tf_op | source)
XLA Modules:
  0.0 154.2 jit_solution(9553394792113601648)
XLA Ops:
  0.6 1.3 broadcast_in_dim.18.fgain_in
  1.9 1.3 broadcast_in_dim.19.lgain_in
  3.2 147.0 %head_window.1 = (bf16[256,1024]{1,0:T(8,128)(2,1)}, bf16[256,1024]{1,0:T(8,128)(2,1)}, bf16[256,1024]{1,0:T(8,128)(2,1)}, bf16[256,1024]{1,0:T(8,128)(2,1)}, bf...) custom-call(bf16[1,256,1536]{2,1,0:T(8,128)(2,1)} %feat_in.1, bf16[64,1536]{1,0:T(8,128)(2,1)} %lat0_in.1, ...), custom_call_target="tpu_custom_call" | custom-call | tf_op jit(solution)/shard_map/head_window/pallas_call | solution.py:798
  150.2 2.6 %results.1 = (bf16[256,1024]{1,0:T(8,128)(2,1)}, bf16[256,1024]{1,0:T(8,128)(2,1)}, bf16[256,1024]{1,0:T(8,128)(2,1)}, bf16[256,1024]{1,0:T(8,128)(2,1)}, bf16[256,1024]{1,0:T(8,128)(2,1)}) custom-call(bf16[256,1024]{1,0:T(8,128)(2,1)} %get-tuple-element.17.refs_0_, bf16[256,1024]{1,0:T(8,128)(2,1)} %get-tuple-element.18.refs_1_, ...), custom_call_target="tpu_custom_call" | custom-call | tf_op jit(solution)/shard_map/results/pallas_call | solution.py:811
  152.8 1.4 copy.26

commit v3 on v2

--- a/solution.py
+++ b/solution.py
@@ -434,7 +434,7 @@
             fn(lax.rem(vi + o, nv))
 
     peers(lambda p: lat_copy(p).start())
-    for a in range(5):
+    for a in range(2):
         peers(lambda p: in_copy(a, p).start())
     for c in wcopies:
         c.start()
@@ -447,8 +447,11 @@
 
     for c in smalls:
         c.wait()
-    f_norm = normed(feat[0], fgain[...])
-    l_norm = normed(lat0[...], lgain[...])
+    def flat(gain):
+        return jnp.concatenate([gain[c : c + 1, :] for c in range(wide // 128)], axis=1)
+
+    f_norm = normed(feat[0], flat(fgain))
+    l_norm = normed(lat0[...], flat(lgain))
     rq = mm(l_norm, wq[...]).astype(BF16)
     rkf = mm(f_norm, wk[...]).astype(BF16)
     rkl = mm(l_norm, wk[...]).astype(BF16)
@@ -516,6 +519,8 @@
         )
 
     peers(lambda p: (x_copy(0, p).start(), x_copy(1, p).start()))
+    for a in range(2, 5):
+        peers(lambda p: in_copy(a, p).start())
     xk[slot_of(me), :] = xk_loc[:, head_of(me)]
     xv[slot_of(me), :] = xv_loc[:, head_of(me)]
 
@@ -657,7 +662,7 @@
     wait_in(4)
 
     def self_step(b, carry):
-        i = nc - 1 - b
+        i = lax.rem(me + 1 + b, nc)
         r = rows_of(i)
         chunks = i // 2 + 1
         qi, gi = q[r, :], g[r, :]
@@ -673,6 +678,14 @@
             return acc + mm(ds, k[cols, :])
 
         gq_s[r, :] = (lax.fori_loop(0, chunks, pass3, zero) * scale).astype(BF16)
+        send(1, i)
+        return carry
+
+    lax.fori_loop(0, nc, self_step, 0)
+
+    def back_step(b, carry):
+        i = lax.rem(me + 1 + b, nc)
+        r = rows_of(i)
         dvi = dv[r, :]
         gk_s[r, :] = (dk[r, :] * scale).astype(BF16)
         gv_s[r, :] = dvi.astype(BF16)
@@ -689,7 +702,7 @@
         send(4, i)
         return carry
 
-    lax.fori_loop(0, nc, self_step, 0)
+    lax.fori_loop(0, nc, back_step, 0)
 
     gxk_s[...] = gxk[...].astype(BF16)
     gxv_s[...] = gxv[...].astype(BF16)
@@ -709,7 +722,6 @@
 
     peers(lambda p: (gx_copy(0, p).start(), gx_copy(1, p).start()))
     send_o = lambda a: (o_local(a).start(), peers(lambda p: o_copy(a, p).start()))
-    send_o(1)
     send_o(2)
     own_k[:, head_of(me)] = gxk_s[slot_of(me), :]
     own_v[:, head_of(me)] = gxv_s[slot_of(me), :]
@@ -762,11 +774,12 @@
     vmem = pl.BlockSpec(memory_space=pltpu.VMEM)
     hbm = pl.BlockSpec(memory_space=pltpu.HBM)
     tok = jax.ShapeDtypeStruct((rows, cols), BF16)
+    lat_t = jax.ShapeDtypeStruct((1, slots, cut), BF16)
     V = pltpu.VMEM
     dma = pltpu.SemaphoreType.DMA
     scratch = (
         [V((1,) + feat.shape[1:], BF16), V((slots, wide), BF16)]
-        + [V((1, wide), F32)] * 2
+        + [V((wide // 128, 128), F32)] * 2
         + [V(wq.shape, BF16)] * 3
         + [V(wo.shape, BF16)]
         + [V((1, nc), jnp.int32), V((1, total), jnp.int32), V((1, nc), F32)]
@@ -797,7 +810,7 @@
     )
     got = pl.pallas_call(
         functools.partial(head_kernel, nc, nv),
-        out_shape=[tok] * 5 + [jax.ShapeDtypeStruct((1, slots, cut), BF16)],
+        out_shape=[tok] * 5 + [lat_t],
         in_specs=[hbm] * 19,
         out_specs=[hbm] * 5 + [vmem],
         scratch_shapes=scratch,
@@ -805,27 +818,28 @@
             collective_id=0, has_side_effects=True, vmem_limit_bytes=62 * 1024 * 1024
         ),
         name="head_window",
-    )(feat, lat0, fgain[None], lgain[None], wq, wk, wv, wo, xwk, xwv, slot_image[None],
+    )(feat, lat0, fgain.reshape(-1, 128), lgain.reshape(-1, 128), wq, wk, wv, wo, xwk, xwv, slot_image[None],
       segments[None], latest_image[None], cross_gate[None], cross_query, self_query, self_key,
       self_value, grad_output)
     moved = pl.pallas_call(
         copy_kernel,
-        out_shape=[tok] * 5,
-        in_specs=[hbm] * 5,
-        out_specs=[hbm] * 5,
-        scratch_shapes=[V(tok.shape, BF16)] * 5 + [dma((2, 5))],
+        out_shape=[tok] * 5 + [lat_t],
+        in_specs=[hbm] * 6,
+        out_specs=[hbm] * 6,
+        scratch_shapes=[V(t.shape, BF16) for t in [tok] * 5 + [lat_t]] + [dma((2, 6))],
         name="results",
-    )(*got[:5])
-    return (*moved, got[5])
+    )(*got)
+    return moved
 
 
 def copy_kernel(*refs):
-    src, dst, held, sem = refs[:5], refs[5:10], refs[10:15], refs[15]
-    first = [pltpu.make_async_copy(src[a], held[a], sem.at[0, a]) for a in range(5)]
-    second = [pltpu.make_async_copy(held[a], dst[a], sem.at[1, a]) for a in range(5)]
+    n = (len(refs) - 1) // 3
+    src, dst, held, sem = refs[:n], refs[n : 2 * n], refs[2 * n : 3 * n], refs[3 * n]
+    first = [pltpu.make_async_copy(src[a], held[a], sem.at[0, a]) for a in range(n)]
+    second = [pltpu.make_async_copy(held[a], dst[a], sem.at[1, a]) for a in range(n)]
     for c in first:
         c.start()
-    for a in range(5):
+    for a in range(n):
         first[a].wait()
         second[a].start()
     for c in second:

time: 155 us -> 140 us (0.903)
  Pallas kernels: 150 us -> 138 us
  local copies, waits for them, and re-layouts: 4.01 us -> 0 us
    pallas_call x1, Pallas kernels: 147 us -> 136 us  [by_head(): pl.pallas_call(functools.partial(head_kernel, nc, nv), out_shape=[tok] *...]
    broadcast_in_dim x2 -> x0, local copies, waits for them, and re-layouts: 2.59 us -> none  [the longest x1 1.3 us: by_head(): fgain[None]]
where the time goes in v3:
time: 140 us; the launch traced here: 139 us
  Pallas kernels  138 us (99%)
    pallas_call x1, Pallas kernels, by_head(): pl.pallas_call(functools.partial(head_kernel, nc, nv), out_shape=[tok] *...  136 us

profile of v3, /device:TPU:0, one launch (start us, length us, event | category | flops | bytes accessed | tf_op | source)
XLA Modules:
  0.0 139.1 jit_solution(864284654248125939)
XLA Ops:
  0.6 135.8 %head_window.1 = (bf16[256,1024]{1,0:T(8,128)(2,1)}, bf16[256,1024]{1,0:T(8,128)(2,1)}, bf16[256,1024]{1,0:T(8,128)(2,1)}, bf16[256,1024]{1,0:T(8,128)(2,1)}, bf...) custom-call(bf16[1,256,1536]{2,1,0:T(8,128)(2,1)} %feat_in.1, bf16[64,1536]{1,0:T(8,128)(2,1)} %lat0_in.1, ...), custom_call_target="tpu_custom_call" | custom-call | tf_op jit(solution)/shard_map/head_window/pallas_call | solution.py:811
  136.4 2.6 %results.1 = (bf16[256,1024]{1,0:T(8,128)(2,1)}, bf16[256,1024]{1,0:T(8,128)(2,1)}, bf16[256,1024]{1,0:T(8,128)(2,1)}, bf16[256,1024]{1,0:T(8,128)(2,1)}, bf16[2...) custom-call(bf16[256,1024]{1,0:T(8,128)(2,1)} %get-tuple-element.12.refs_0_, ...), custom_call_target="tpu_custom_call" | custom-call | tf_op jit(solution)/shard_map/results/pallas_call | solution.py:824
